TPU v7x, 128 devices: a whole 4x4x4 slice. The times are simulated.
128 devices in a mesh: dp: 4 (over z), spatial: 16 (over y_hi, x, core), fsdp: 2 (over y_lo).
Axes of the slice: x: 4, y: 4 (y_hi: 2, y_lo: 2; y = y_hi * 2 + y_lo), z: 4, core: 2. Of those that a mesh axis runs over, the one named last changes fastest.
Arguments:
- features: bfloat16 [8, 128, 256, 256], P(('dp', 'fsdp'), 'spatial'), may hold values from -6 to 6
- geometry: int32 [8, 128, 256], P(('dp', 'fsdp'), 'spatial'), may hold values from 0 to 2
- bc_class: int32 [8], P(('dp', 'fsdp')), may hold values from 0 to 7, as said below
- code_scale: float32 [3, 256], replicated, may hold values from 0.5 to 2
- bc_bias: float32 [8, 256], replicated, may hold values from -3 to 3
- kernel_one: bfloat16 [3, 3, 256, 256], P(None, None, None, 'fsdp'), may hold values from -0.125 to 0.125
- kernel_two: bfloat16 [3, 3, 256, 256], P(None, None, None, 'fsdp'), may hold values from -0.125 to 0.125
- cotangent: bfloat16 [8, 128, 256, 256], P(('dp', 'fsdp'), 'spatial'), may hold values from -6 to 6
Outputs:
- grad_features: bfloat16 [8, 128, 256, 256], P(('dp', 'fsdp'), 'spatial')
- grad_one: float32 [3, 3, 256, 256], P(None, None, None, 'fsdp')
- grad_two: float32 [3, 3, 256, 256], P(None, None, None, 'fsdp')
Inputs may be any that keep to these rules, and one draw needn't show every extreme that they name: `bc_class`: every class occurs among the samples.
All inputs are finite; a program needn't handle non-finite values.
Results may differ from a plain program's by a relative error of at most 0.0065.
Values may be sent and summed in bfloat16 or wider, within the bound.
A program may use at most 64 MiB of HBM per device.

v0:
```python
import math

import jax
import jax.numpy as jnp
from jax import lax
from jax.sharding import PartitionSpec as P

NB = 8


def padded_2(block, sides, width):
    for axis, dim in sides:
        count = lax.axis_size(axis)
        forward = [(i, i + 1) for i in range(count - 1)]
        backward = [(target, source) for source, target in forward]
        low = lax.ppermute(
            lax.slice_in_dim(block, block.shape[dim] - width, None, axis=dim), axis, forward
        )
        high = lax.ppermute(lax.slice_in_dim(block, 0, width, axis=dim), axis, backward)
        block = jnp.concatenate([low, block, high], axis=dim)
    return block


def conv_rows(padded, kernel):
    return lax.conv_general_dilated(
        padded,
        kernel,
        (1, 1),
        ((0, 0), (1, 1)),
        dimension_numbers=("NHWC", "HWIO", "NHWC"),
        preferred_element_type=jnp.float32,
    )


def flipped(kernel):
    return jnp.transpose(kernel[::-1, ::-1], (0, 1, 3, 2))


def whole_kernel(kernel):
    return lax.all_gather(kernel, "fsdp", axis=3, tiled=True)


def correlate(padded, grads):
    height = grads.shape[1]
    width = grads.shape[2]
    wide = jnp.pad(padded, ((0, 0), (0, 0), (1, 1), (0, 0)))
    rows_out = []
    for row_off in range(3):
        cols_out = []
        for col_off in range(3):
            window = wide[:, row_off : row_off + height, col_off : col_off + width, :]
            cols_out.append(
                jnp.einsum("nhwc,nhwo->co", window, grads, preferred_element_type=jnp.float32)
            )
        rows_out.append(jnp.stack(cols_out))
    return jnp.stack(rows_out)


def reduce_grad(local_grad, factor):
    summed = lax.psum(local_grad, ("dp", "spatial"))
    mine = lax.psum_scatter(summed, "fsdp", scatter_dimension=3, tiled=True)
    return mine * factor


def on_device(features, geometry, bc_class, code_scale, bc_bias, kernel_one, kernel_two, cotangent):
    rows = features.shape[1]
    width = features.shape[2]
    slabs = lax.axis_size("spatial")
    gain = jnp.zeros(features.shape, jnp.float32)
    for code in range(3):
        gain = gain + (geometry == code).astype(jnp.float32)[..., None] * code_scale[code]
    onehot = (bc_class[:, None] == jnp.arange(NB, dtype=jnp.int32)[None, :]).astype(jnp.float32)
    offset = jnp.dot(onehot, bc_bias, precision=lax.Precision.HIGHEST)
    gated = (features.astype(jnp.float32) * gain + offset[:, None, None, :]).astype(jnp.bfloat16)
    full_one = whole_kernel(kernel_one)
    full_two = whole_kernel(kernel_two)
    stacked = jnp.stack([gated, cotangent])
    padded_both = padded_2(stacked, (("spatial", 2),), 1)
    gated_pad = padded_both[0]
    cot_pad = padded_both[1]
    pre = conv_rows(gated_pad, full_one)
    act = jax.nn.gelu(pre).astype(jnp.bfloat16)
    act_pad = padded_2(act, (("spatial", 1),), 1)
    grad_act = conv_rows(cot_pad, flipped(full_two))
    grad_pre = jax.vjp(jax.nn.gelu, pre)[1](grad_act)[0].astype(jnp.bfloat16)
    grad_pad = padded_2(grad_pre, (("spatial", 1),), 1)
    back = cotangent.astype(jnp.float32) + conv_rows(grad_pad, flipped(full_one))
    grad_features = (back * gain).astype(jnp.bfloat16)
    total_cells = (
        features.shape[0] * lax.axis_size("dp") * lax.axis_size("fsdp") * rows * slabs * width
    )
    factor = 1.0 / math.sqrt(total_cells)
    grad_two = reduce_grad(correlate(act_pad, cotangent), factor)
    grad_one = reduce_grad(correlate(gated_pad, grad_pre), factor)
    return (grad_features, grad_one, grad_two)


def solution(mesh):
    placed = (
        P(("dp", "fsdp"), "spatial", None, None),
        P(("dp", "fsdp"), "spatial", None),
        P(("dp", "fsdp")),
        P(),
        P(),
        P(None, None, None, "fsdp"),
        P(None, None, None, "fsdp"),
        P(("dp", "fsdp"), "spatial", None, None),
    )
    return jax.shard_map(
        on_device,
        mesh=mesh,
        in_specs=placed,
        out_specs=(
            P(("dp", "fsdp"), "spatial", None, None),
            P(None, None, None, "fsdp"),
            P(None, None, None, "fsdp"),
        ),
        check_vma=False,
    )
```

profile of v0, /device:TPU:1, one launch (start us, length us, event | category | flops | bytes accessed | tf_op | source)
XLA Modules:
  0.0 810.3 jit_solution(14092664318965314654)
XLA Ops:
  9.4 1.5 copy.15
  12.4 4.5 collective-permute-start
  16.9 1.9 collective-permute-start.1
  20.2 4.4 collective-permute-done.1
  25.0 2.2 slice_bitcast_fusion.2
  27.2 1.6 copy.45
  30.3 2.3 reshape.162
  34.0 1.6 copy.44
  37.0 2.5 reshape.157
  41.6 6.3 multiply_convert_fusion
  48.0 20.6 %all-gather.3.cloned.1.call-done = bf16[3,3,256,256]{3,2,1,0:T(8,128)(2,1)} async-done(((bf16[3,3,256,128]{3,2,1,0:T(8,128)(2,1)}), bf16[3,3,256,256]{3,2,1,0:T(8,128)(2,1)}) %all-gather.3.cloned.1.call-update) | async-done | bytes 1179664 | tf_op jit(solution)/shard_map/all_gather | solution.py:40
  68.6 6.0 fusion.13
  82.3 1.6 pad_maximum_fusion.1
  85.2 1.7 copy.42
  90.4 3.6 collective-permute-start.4
  94.2 1.9 collective-permute-start.5
  96.6 4.3 collective-permute-done.5
  101.4 2.1 fusion.17
  108.2 1.6 pad_maximum_fusion.2
  109.8 13.8 %reduce-scatter.3.cloned.1.call-done = f32[3,3,256,128]{3,2,1,0:T(8,128)} async-done(((f32[3,3,256,256]{3,2,1,0:T(8,128)}), f32[3,3,256,128]{3,2,1,0:T(8,128)}) %reduce-scatter.3.cloned.1.call-update) | async-done | bytes 1179664 | tf_op jit(solution)/shard_map/reduce_scatter | solution.py:61
  123.7 40.3 %reduce-scatter.5.cloned.1.call-done = f32[3,3,256,128]{3,2,1,0:T(8,128)} async-done(((f32[3,3,256,256]{3,2,1,0:T(8,128)}), f32[3,3,256,128]{3,2,1,0:T(8,128)}) %reduce-scatter.5.cloned.1.call-update) | async-done | bytes 1179664 | tf_op jit(solution)/shard_map/reduce_scatter | solution.py:61
  165.1 3.7 collective-permute-start.2
  169.0 1.9 collective-permute-start.3
  171.1 4.1 collective-permute-done.3
  176.8 2.3 reshape.179
  180.4 2.8 convolution_select_fusion
  183.9 1.5 slice.145
  185.4 1.9 copy.40
  187.3 1.7 fusion.15
  189.0 2.3 copy.38
  191.3 608.9 %all-reduce.5.cloned.1.call-done = (f32[3,3,256,128]{3,2,1,0:T(8,128)}, f32[3,3,256,128]{3,2,1,0:T(8,128)}) async-done(((f32[3,3,256,128]{3,2,1,0:T(8,128)}, f32[3,3,256,128]{3,2,1,0:T(8,128)}), (f32[3,3,256,128]{3,2,1,0:T(8,128)}, f32[3,3,256,128]{3,2,1,0:T(8,128)})) %all-reduce.5.cloned.1.call-update) | async-done | bytes 2359312 | tf_op jit(solution)/shard_map/psum | solution.py:60
  800.2 2.5 broadcast_multiply_fusion.1
  (108 shorter events, 35.3 us)
Async XLA Ops:
  7.2 4.3 copy-start
  7.2 3.7 copy-start.12
  7.2 34.5 %all-gather.5.cloned.1.call-start = ((), (), s32[]{:S(2)}) async-start(), calls=%async_computation.3 | async-start | bytes 1769472 | tf_op jit(solution)/shard_map/all_gather | solution.py:40
  7.9 60.7 %all-gather.3.cloned.1.call-start = ((), (), s32[]{:S(2)}) async-start(), calls=%async_computation.2 | async-start | bytes 1769472 | tf_op jit(solution)/shard_map/all_gather | solution.py:40
  9.4 2.2 copy-start.13
  12.4 7.8 collective-permute-start
  16.9 7.7 collective-permute-start.1
  18.9 104.8 %reduce-scatter.3.cloned.1.call-start = ((), (), s32[]{:S(2)}) async-start(), calls=%async_computation.4 | async-start | bytes 3538944 | tf_op jit(solution)/shard_map/reduce_scatter | solution.py:61
  32.9 1.1 copy-start.7
  39.5 2.1 copy-start.15
  39.8 1.2 copy-start.8
  41.6 27.0 %copy-start.9 = (bf16[10,1,8,33,256]{4,2,3,0,1:T(8,128)(2,1)S(1)}, bf16[10,1,8,33,256]{4,2,3,0,1:T(8,128)(2,1)}, u32[]{:S(2)}) copy-start(bf16[10,1,8,33,256]{4,2,3,0,1:T(8,128)(2,1)} %copy-done.8) | copy-start | bytes 4055044
  48.0 36.0 %copy-start.6 = (bf16[8,8,33,256]{3,1,2,0:T(8,128)(2,1)}, bf16[8,8,33,256]{3,1,2,0:T(8,128)(2,1)S(1)}, u32[]{:S(2)}) copy-start(bf16[8,8,33,256]{3,1,2,0:T(8,128)(2,1)S(1)} %get-tuple-element.26) | copy-start | bytes 3244036
  74.6 1.0 copy-start.5
  74.6 1.7 copy-start.10
  75.6 6.0 copy-start.3
  83.9 80.0 %reduce-scatter.5.cloned.1.call-start = ((), (), s32[]{:S(2)}) async-start(), calls=%async_computation.5 | async-start | bytes 3538944 | tf_op jit(solution)/shard_map/reduce_scatter | solution.py:61
  85.2 11.0 %copy-start.2 = (bf16[1,8,256,256]{3,2,1,0:T(8,128)(2,1)S(1)}, bf16[1,8,256,256]{3,2,1,0:T(8,128)(2,1)}, u32[]{:S(2)}) copy-start(bf16[1,8,256,256]{3,2,1,0:T(8,128)(2,1)} %param.15) | copy-start | bytes 3145732
  90.4 11.0 %collective-permute-start.4 = (bf16[1,1,256,256]{2,3,1,0:T(8,128)(2,1)}, bf16[1,1,256,256]{2,3,1,0:T(8,128)(2,1)}, u32[]{:S(2)}, u32[]{:S(2)}) collective-permute-start(bf16[1,1,256,256]{2,3,1,0:T(8,128)(2,1)} %copy.41), channel_id=1, source_target_pairs={{0,2},{2,4},{4,6},{6,8},{8,10},{10,12},{12,14},{14,16},{16,18},{18... | collective-permute-start | bytes 393224 | tf_op jit(solution)/shard_map/ppermute | solution.py:16
  94.2 6.7 collective-permute-start.5
  109.8 690.4 %all-reduce.5.cloned.1.call-start = ((), (), s32[]{:S(2)}) async-start(), calls=%async_computation.6 | async-start | bytes 4718592 | tf_op jit(solution)/shard_map/psum | solution.py:60
  163.9 7.0 copy-start.4
  165.1 6.0 collective-permute-start.2
  169.0 6.3 collective-permute-start.3
  179.1 1.3 copy-start.14
  800.2 2.5 copy-start.11
  800.2 3.6 copy-start.1
Sparse Core Ops, SparseCore 0:
  9.7 28.4 all-gather.4
  39.8 28.7 all-gather.2
  84.0 39.6 reduce-scatter.2
  126.0 37.8 reduce-scatter.4
  166.3 633.8 all-reduce.4
where the time goes:
time: 814 us; the launch traced here: 810 us
  waiting for transfers between devices  698 us (86%)
  local copies, waits for them, and re-layouts  40.4 us (5%)
  matrix products  26.2 us (3%)
  starting transfers between devices  17.8 us (2%)
  between operations  15.1 us (2%)
  other arithmetic  12.3 us (2%)
    psum x1, waiting for transfers between devices, reduce_grad(): summed = lax.psum(local_grad, ('dp', 'spatial'))  609 us
    reduce_scatter x2, waiting for transfers between devices, reduce_grad(): mine = lax.psum_scatter(summed, 'fsdp', scatter_dimension=3, tiled=True)  54.1 us
    all_gather x2, waiting for transfers between devices, whole_kernel(): return lax.all_gather(kernel, 'fsdp', axis=3, tiled=True)  20.6 us
  transfers between devices with their start and end apart: 11, of which 8 were waited for; matrix products, arithmetic and copies ran while one was open for 7% of the time, Pallas kernels for 0%

commit v1 on v0

v1 whole, which is shorter than its diff:
```python
import functools
import math

import jax
import jax.numpy as jnp
from jax import lax
from jax.experimental import pallas as pl
from jax.experimental.pallas import tpu as pltpu
from jax.sharding import PartitionSpec as P

MESH = pl.DeviceIdType.MESH
BF, F32 = jnp.bfloat16, jnp.float32
ROWS, WIDTH, C, HALF = 8, 256, 256, 128
CELLS = ROWS * WIDTH
QUARTER = 9 * C // 4
NN = (((1,), (0,)), ((), ()))
NT = (((1,), (1,)), ((), ()))
TN = (((0,), (0,)), ((), ()))
PIECES = 6
LINE_AXIS = ("z", "x", "z", "x", "z", "x")
SLOPE = math.sqrt(2.0 / math.pi)


def dot(a, b, dims):
    return lax.dot_general(a, b, dims, preferred_element_type=F32)


def put_shifted(value, low_ref, mid_ref, high_ref):
    place = lax.broadcasted_iota(jnp.int32, value.shape, 0)
    low_ref[...] = jnp.where(place == 0, 0.0, pltpu.roll(value, 1, 0)).astype(BF)
    mid_ref[...] = value.astype(BF)
    high_ref[...] = jnp.where(place == WIDTH - 1, 0.0, pltpu.roll(value, WIDTH - 1, 0)).astype(BF)


def body(
    feat, geo, bc, scale, bias, k1, k2, cot, gf, grads,
    fbuf, cbuf, gbuf, geot, sbuf, bbuf, gated_halo, cot_halo, pre_halo, edge,
    xg, xc, xp, w1, w2, pre, gact, act, part,
    sib_out, sib_in, plane_out, plane_in, line_out, line_in, shard,
    load_sem, halo_send, halo_recv, w_send, w_recv, r_send, r_recv,
):
    dp = lax.axis_index("dp")
    sp = lax.axis_index("spatial")
    fs = lax.axis_index("fsdp")
    core, cx, yh = sp % 2, (sp // 2) % 4, sp // 8
    cy = yh * 2 + fs
    other = 1 - fs

    def device(x, y, z, c):
        return (z, ((y // 2) * 4 + x) * 2 + c, y % 2)

    sibling = device(cx, cy, dp, 1 - core)
    up, down = (dp, sp - 1, fs), (dp, sp + 1, fs)
    has_up, has_down = sp > 0, sp < 15

    def peer(axis, k):
        side = k // 4
        y = (cy + k % 4) % 4
        if axis == "z":
            return (cx + side) % 4, y, dp
        return cx, y, (dp + side) % 4

    barrier = pltpu.get_barrier_semaphore()

    def greet(target):
        pl.semaphore_signal(barrier, inc=1, device_id=target, device_id_type=MESH)

    greet(sibling)
    pl.when(jnp.logical_and(core == 0, has_up))(lambda: greet(up))
    pl.when(jnp.logical_and(core == 1, has_down))(lambda: greet(down))

    def greet_z(k, _):
        greet(device(*peer("z", k), core))
        return 0

    def greet_x(k, _):
        greet(device(*peer("x", k), core))
        return 0

    lax.fori_loop(1, 16, greet_z, 0)
    lax.fori_loop(4, 16, greet_x, 0)

    def load(src, dst, i):
        cp = pltpu.make_async_copy(src, dst, load_sem.at[i])
        cp.start()
        return cp

    geo_cp = load(geo, gbuf, 0)
    scale_cp = load(scale, sbuf, 1)
    bias_cp = load(bias, bbuf, 2)
    feat_cp = load(feat, fbuf, 3)
    cot_cp = load(cot, cbuf, 4)
    k2_cp = load(k2, w2.at[fs], 5)
    k1_cp = load(k1, w1.at[fs], 6)

    strangers = jnp.where(core == 0, jnp.where(has_up, 1, 0), jnp.where(has_down, 1, 0))
    pl.semaphore_wait(barrier, 28 + strangers)

    def remote(src, dst, send, recv, target):
        return pltpu.make_async_remote_copy(
            src_ref=src, dst_ref=dst, send_sem=send, recv_sem=recv, device_id=target, device_id_type=MESH
        )

    def halo_up(src, n, buf):
        return remote(src, buf.at[1], halo_send.at[n, 0], halo_recv.at[n, 1], up)

    def halo_down(src, n, buf):
        return remote(src, buf.at[0], halo_send.at[n, 1], halo_recv.at[n, 0], down)

    top, bottom = pl.ds(0, WIDTH), pl.ds(CELLS - WIDTH, WIDTH)
    cot_up = halo_up(cot.at[top], 0, cot_halo)
    cot_down = halo_down(cot.at[bottom], 0, cot_halo)
    gated_up = halo_up(edge.at[0], 1, gated_halo)
    gated_down = halo_down(edge.at[1], 1, gated_halo)
    pre_up = halo_up(xp.at[pl.ds(WIDTH, WIDTH), pl.ds(C, C)], 2, pre_halo)
    pre_down = halo_down(xp.at[pl.ds(CELLS, WIDTH), pl.ds(C, C)], 2, pre_halo)
    pl.when(has_up)(lambda: cot_up.start())
    pl.when(has_down)(lambda: cot_down.start())

    next_a = device(cx, yh * 2 + other, dp, core)
    next_b = device(cx, (1 - yh) * 2 + other, dp, core)

    def quarter_copies(i, src, w):
        out = []
        for side, target in ((0, next_a), (1, next_b)):
            at = pl.ds(pl.multiple_of((2 * core + side) * QUARTER, 16), QUARTER)
            out.append(remote(src.at[at], w.at[fs, at], w_send.at[i, side], w_recv.at[i, side], target))
        at = pl.ds(pl.multiple_of(2 * core * QUARTER, 16), 2 * QUARTER)
        out.append(remote(w.at[other, at], w.at[other, at], w_send.at[i, 2], w_recv.at[i, 2], sibling))
        return out

    w1_copies = quarter_copies(0, k1, w1)
    w2_copies = quarter_copies(1, k2, w2)
    for cp in w1_copies[:2] + w2_copies[:2]:
        cp.start()

    geo_cp.wait()
    geot[...] = jnp.transpose(gbuf[...])
    scale_cp.wait()
    bias_cp.wait()
    classes = lax.broadcasted_iota(jnp.int32, (8, C), 0)
    offset = jnp.sum(jnp.where(classes == bc[0], bbuf[...], 0.0), axis=0, keepdims=True)

    def gain_of(row):
        code = geot[:, row : row + 1]
        return jnp.where(
            code == 0, sbuf[0:1, :], jnp.where(code == 1, sbuf[1:2, :], sbuf[2:3, :])
        )

    def put_row(x, r, value):
        at = pl.ds(r * WIDTH, WIDTH)
        put_shifted(value, x.at[at, pl.ds(0, C)], x.at[at, pl.ds(C, C)], x.at[at, pl.ds(2 * C, C)])

    def gated_row(row):
        f = fbuf[row * WIDTH : (row + 1) * WIDTH, :].astype(F32)
        return f * gain_of(row) + offset

    feat_cp.wait()
    first, last = gated_row(0), gated_row(ROWS - 1)
    edge[0] = first.astype(BF)
    edge[1] = last.astype(BF)
    pl.when(has_up)(lambda: gated_up.start())
    pl.when(has_down)(lambda: gated_down.start())
    for row in range(ROWS):
        put_row(xg, row + 1, gated_row(row))

    def put_cot(r, value):
        at = pl.ds(r * WIDTH, WIDTH)
        for h in range(2):
            put_shifted(
                value[:, h * HALF : (h + 1) * HALF],
                xc.at[h, at, pl.ds(0, HALF)],
                xc.at[h, at, pl.ds(HALF, HALF)],
                xc.at[h, at, pl.ds(2 * HALF, HALF)],
            )

    cot_cp.wait()
    for row in range(ROWS):
        put_cot(row + 1, cbuf[row * WIDTH : (row + 1) * WIDTH, :].astype(F32))

    def grad_act_half(h, r, rows):
        lhs = jnp.concatenate([xc[h, pl.ds((r + d) * WIDTH, rows * WIDTH), :] for d in range(3)], axis=1)
        rhs = jnp.concatenate([w2[h, (8 - t) * C : (9 - t) * C, :] for t in range(9)], axis=1)
        return dot(lhs, rhs, NT)

    k2_cp.wait()
    for r in (2, 4):
        gact[r * WIDTH : (r + 2) * WIDTH, :] = grad_act_half(fs, r, 2)

    def halo_rows(up_copy, down_copy, buf, put):
        @pl.when(has_up)
        def _():
            down_copy.wait_recv()
            put(0, buf[0].astype(F32))

        @pl.when(jnp.logical_not(has_up))
        def _():
            put(0, jnp.zeros((WIDTH, C), F32))

        @pl.when(has_down)
        def _():
            up_copy.wait_recv()
            put(ROWS + 1, buf[1].astype(F32))

        @pl.when(jnp.logical_not(has_down))
        def _():
            put(ROWS + 1, jnp.zeros((WIDTH, C), F32))

    halo_rows(cot_up, cot_down, cot_halo, put_cot)
    for r in (0, 6):
        gact[r * WIDTH : (r + 2) * WIDTH, :] = grad_act_half(fs, r, 2)
    for cp in w1_copies[:2]:
        cp.wait_recv()
    w1_copies[2].start()
    halo_rows(gated_up, gated_down, gated_halo, functools.partial(put_row, xg))
    k1_cp.wait()
    w1_copies[2].wait_recv()

    def big_lhs(x, r, rows):
        return jnp.concatenate([x[pl.ds((r + d) * WIDTH, rows * WIDTH), :] for d in range(3)], axis=1)

    pre[...] = dot(big_lhs(xg, 0, ROWS), jnp.concatenate([w1[0], w1[1]], axis=1), NN)
    for cp in w2_copies[:2]:
        cp.wait_recv()
    w2_copies[2].start()

    def act_row(row, _):
        at = pl.ds(pl.multiple_of(row * WIDTH, WIDTH), WIDTH)
        v = pre[at, :]
        act[at, :] = (0.5 * v * (1.0 + jnp.tanh(SLOPE * (v + 0.044715 * (v * v * v))))).astype(BF)
        return 0

    lax.fori_loop(0, ROWS, act_row, 0)

    def sib_copy(p):
        return remote(sib_out.at[p], sib_in.at[p], r_send.at[p, 0], r_recv.at[p, 0], sibling)

    def mine(p, source):
        return source[p, :, pl.ds(pl.multiple_of(core * HALF, HALF), HALF), :]

    def stage1(p):
        sib_out[p] = part[p, :, pl.ds(pl.multiple_of((1 - core) * HALF, HALF), HALF), :].astype(BF)
        sib_copy(p).start()

    def plane_wait(p):
        return remote(plane_in.at[p], plane_in.at[p], r_send.at[p, 1], r_recv.at[p, 1], sibling)

    def slot_of(x, y, z, axis):
        return (x if axis == "z" else z) * 4 + y

    def stage2(p):
        axis = LINE_AXIS[p]
        sib_copy(p).wait_recv()
        total = mine(p, part) + sib_in[p].astype(F32)
        for block in range(8):
            for h in range(2):
                plane_out[p, block * 2 + h] = total[
                    :, block * 16 : (block + 1) * 16, h * HALF : (h + 1) * HALF
                ].astype(BF)

        def send(k, _):
            to = peer(axis, k)
            remote(
                plane_out.at[p, slot_of(*to, axis)], plane_in.at[p, k - 1],
                r_send.at[p, 1], r_recv.at[p, 1], device(*to, core),
            ).start()
            return 0

        lax.fori_loop(1, 16, send, 0)

    def line_wait(p):
        return remote(line_in.at[p], line_in.at[p], r_send.at[p, 2], r_recv.at[p, 2], sibling)

    def stage3(p):
        axis = LINE_AXIS[p]
        plane_wait(p).wait_recv()
        total = plane_out[p, slot_of(cx, cy, dp, axis)].astype(F32)
        for k in range(15):
            total = total + plane_in[p, k].astype(F32)
        line_out[p] = total.astype(BF)

        def send(k, _):
            to = (cx, cy, (dp + k) % 4) if axis == "z" else ((cx + k) % 4, cy, dp)
            remote(
                line_out.at[p], line_in.at[p, k - 1], r_send.at[p, 2], r_recv.at[p, 2], device(*to, core)
            ).start()
            return 0

        lax.fori_loop(1, 4, send, 0)

    def row_of(block):
        return pl.ds(pl.multiple_of(core * HALF + block * 16, 16), 16)

    def gather_wait(p):
        few = plane_in.at[p, pl.ds(0, 7)]
        return remote(few, few, r_send.at[p, 3], r_recv.at[p, 3], sibling)

    def stage4(p):
        axis = LINE_AXIS[p]
        line_wait(p).wait_recv()
        total = line_out[p].astype(F32)
        for k in range(3):
            total = total + line_in[p, k].astype(F32)
        shard[p] = total.astype(BF)
        block = (cx if axis == "z" else dp) * 2 + yh
        grads[3 * p : 3 * p + 3, row_of(block), :] = total.astype(BF)

        def send(k, _):
            y = ((yh + k) % 2) * 2 + fs
            to = ((cx + k // 2) % 4, y, dp) if axis == "z" else (cx, y, (dp + k // 2) % 4)
            remote(
                shard.at[p], grads.at[pl.ds(3 * p, 3), row_of(block)],
                r_send.at[p, 3], r_recv.at[p, 3], device(*to, core),
            ).start()
            return 0

        lax.fori_loop(1, 8, send, 0)

    def last_copy(p):
        at = grads.at[pl.ds(3 * p, 3), pl.ds(pl.multiple_of(core * HALF, HALF), HALF)]
        return remote(at, at, r_send.at[p, 4], r_recv.at[p, 4], sibling)

    def stage5(p):
        gather_wait(p).wait_recv()
        last_copy(p).start()

    for d in range(3):
        for e in range(3):
            for h in range(2):
                part[d, e, :, h * HALF : (h + 1) * HALF] = dot(
                    act[...], xc[h, pl.ds((2 - d) * WIDTH, CELLS), (2 - e) * HALF : (3 - e) * HALF], TN
                )
        stage1(d)
        if d >= 1:
            stage2(d - 1)

    w2_copies[2].wait_recv()

    def grad_pre_rows(r):
        at = slice(r * WIDTH, (r + 2) * WIDTH)
        g = gact[at, :] + grad_act_half(other, r, 2)
        v = pre[at, :]
        sq = v * v
        t = jnp.tanh(SLOPE * (v + 0.044715 * (sq * v)))
        slope = 0.5 * (1.0 + t) + 0.5 * v * (1.0 - t * t) * (SLOPE * (1.0 + (3 * 0.044715) * sq))
        g = g * slope
        for i in range(2):
            put_row(xp, r + i + 1, g[i * WIDTH : (i + 1) * WIDTH])

    grad_pre_rows(0)
    pl.when(has_up)(lambda: pre_up.start())
    grad_pre_rows(6)
    pl.when(has_down)(lambda: pre_down.start())
    stage2(2)
    grad_pre_rows(2)
    stage3(0)
    grad_pre_rows(4)
    stage3(1)

    for d in range(3):
        p = 3 + d
        for e in range(3):
            part[p, e] = dot(
                xg[pl.ds(d * WIDTH, CELLS), e * C : (e + 1) * C], xp[pl.ds(WIDTH, CELLS), C : 2 * C], TN
            )
        stage1(p)
        if d == 0:
            stage3(2)
            stage4(0)
        elif d == 1:
            stage2(3)
            stage4(1)
        else:
            stage2(4)
            stage4(2)
            stage5(0)

    halo_rows(pre_up, pre_down, pre_halo, functools.partial(put_row, xp))

    def back_rows(r):
        rhs = jnp.concatenate(
            [jnp.concatenate([w1[0, (8 - t) * C : (9 - t) * C, :], w1[1, (8 - t) * C : (9 - t) * C, :]], axis=1) for t in range(9)],
            axis=1,
        )
        g = dot(big_lhs(xp, r, 2), rhs, NT)
        for i in range(2):
            at = slice((r + i) * WIDTH, (r + i + 1) * WIDTH)
            total = cbuf[at, :].astype(F32) + g[i * WIDTH : (i + 1) * WIDTH]
            fbuf[at, :] = (total * gain_of(r + i)).astype(BF)

    back_rows(0)
    stage2(5)
    stage3(3)
    back_rows(2)
    stage3(4)
    stage5(1)
    back_rows(4)
    stage3(5)
    stage4(3)
    back_rows(6)
    out_cp = pltpu.make_async_copy(fbuf, gf, load_sem.at[3])
    out_cp.start()
    stage4(4)
    stage5(2)
    stage4(5)
    stage5(3)
    stage5(4)
    stage5(5)
    for p in range(PIECES):
        last_copy(p).wait_recv()

    for p in range(PIECES):
        sib_copy(p).wait_send()
        plane_wait(p).wait_send()
        line_wait(p).wait_send()
        gather_wait(p).wait_send()
        last_copy(p).wait_send()
    for cp in w1_copies + w2_copies:
        cp.wait_send()
    for ups, downs in ((cot_up, cot_down), (gated_up, gated_down), (pre_up, pre_down)):
        pl.when(has_up)(lambda ups=ups: ups.wait_send())
        pl.when(has_down)(lambda downs=downs: downs.wait_send())
    out_cp.wait()


def on_device(features, geometry, bc_class, code_scale, bc_bias, kernel_one, kernel_two, cotangent):
    any_spec = pl.BlockSpec(memory_space=pl.ANY)
    vmem = pltpu.VMEM
    dma = pltpu.SemaphoreType.DMA
    grad_features, grads = pl.pallas_call(
        body,
        out_shape=(
            jax.ShapeDtypeStruct((CELLS, C), BF),
            jax.ShapeDtypeStruct((18, C, HALF), BF),
        ),
        in_specs=[any_spec, any_spec, pl.BlockSpec(memory_space=pltpu.SMEM)] + [any_spec] * 5,
        out_specs=(any_spec, pl.BlockSpec(memory_space=pltpu.VMEM)),
        scratch_shapes=[
            vmem((CELLS, C), BF),
            vmem((CELLS, C), BF),
            vmem((ROWS, WIDTH), jnp.int32),
            vmem((WIDTH, ROWS), jnp.int32),
            vmem((3, C), F32),
            vmem((8, C), F32),
            vmem((2, WIDTH, C), BF),
            vmem((2, WIDTH, C), BF),
            vmem((2, WIDTH, C), BF),
            vmem((2, WIDTH, C), BF),
            vmem((CELLS + 2 * WIDTH, 3 * C), BF),
            vmem((2, CELLS + 2 * WIDTH, 3 * HALF), BF),
            vmem((CELLS + 2 * WIDTH, 3 * C), BF),
            vmem((2, 9 * C, HALF), BF),
            vmem((2, 9 * C, HALF), BF),
            vmem((CELLS, C), F32),
            vmem((CELLS, C), F32),
            vmem((CELLS, C), BF),
            vmem((PIECES, 3, C, C), F32),
            vmem((PIECES, 3, HALF, C), BF),
            vmem((PIECES, 3, HALF, C), BF),
            vmem((PIECES, 16, 3, 16, HALF), BF),
            vmem((PIECES, 15, 3, 16, HALF), BF),
            vmem((PIECES, 3, 16, HALF), BF),
            vmem((PIECES, 3, 3, 16, HALF), BF),
            vmem((PIECES, 3, 16, HALF), BF),
            dma((7,)),
            dma((3, 2)),
            dma((3, 2)),
            dma((2, 3)),
            dma((2, 3)),
            dma((PIECES, 5)),
            dma((PIECES, 5)),
        ],
        compiler_params=pltpu.CompilerParams(
            collective_id=0, has_side_effects=True, vmem_limit_bytes=58 * 2**20
        ),
    )(
        features.reshape(CELLS, C),
        geometry.reshape(ROWS, WIDTH),
        bc_class,
        code_scale,
        bc_bias,
        kernel_one.reshape(9 * C, HALF),
        kernel_two.reshape(9 * C, HALF),
        cotangent.reshape(CELLS, C),
    )
    scaled = grads.astype(F32) * (1.0 / math.sqrt(8 * 128 * 256))
    scaled = scaled.reshape(2, 3, 3, C, HALF)
    return grad_features.reshape(features.shape), scaled[1], scaled[0]


def solution(mesh):
    placed = (
        P(("dp", "fsdp"), "spatial", None, None),
        P(("dp", "fsdp"), "spatial", None),
        P(("dp", "fsdp")),
        P(),
        P(),
        P(None, None, None, "fsdp"),
        P(None, None, None, "fsdp"),
        P(("dp", "fsdp"), "spatial", None, None),
    )
    return jax.shard_map(
        on_device,
        mesh=mesh,
        in_specs=placed,
        out_specs=(
            P(("dp", "fsdp"), "spatial", None, None),
            P(None, None, None, "fsdp"),
            P(None, None, None, "fsdp"),
        ),
        check_vma=False,
    )
```

time: 814 us -> 74.3 us (0.09)
  waiting for transfers between devices: 698 us -> 0 us
  Pallas kernels: 0 us -> 68.7 us
  local copies, waits for them, and re-layouts: 40.4 us -> 2.54 us
  matrix products: 26.2 us -> 0 us
  starting transfers between devices: 17.8 us -> 0 us
  between operations: 15.1 us -> 1.3 us
  other arithmetic: 12.3 us -> 1.51 us
    psum x1 -> x0, waiting for transfers between devices: 609 us -> none  [reduce_grad(): summed = lax.psum(local_grad, ('dp', 'spatial'))]
    pallas_call x0 -> x1, Pallas kernels: none -> 68.7 us  [on_device(): pl.pallas_call(body, out_shape=(jax.ShapeDtypeStruct((CELLS, C), BF), jax...]
    reduce_scatter x2 -> x0, waiting for transfers between devices: 54.1 us -> none  [reduce_grad(): mine = lax.psum_scatter(summed, 'fsdp', scatter_dimension=3, tiled=True)]
    all_gather x2 -> x0, waiting for transfers between devices: 20.6 us -> none  [whole_kernel(): return lax.all_gather(kernel, 'fsdp', axis=3, tiled=True)]
    ppermute x6 -> x0, starting transfers between devices: 17.6 us -> none  [the longest x3 11.8 us: padded_2(): lax.ppermute(lax.slice_in_dim(block, block.shape[dim] - width, None, axis...]
    unnamed x42 -> x3, local copies, waits for them, and re-layouts: 16.1 us -> 0.99 us
    conv_general_dilated x3 -> x0, matrix products: 15.1 us -> none  [conv_rows(): lax.conv_general_dilated(padded, kernel, (1, 1), ((0, 0), (1, 1)), dimens...]
    ppermute x6 -> x0, waiting for transfers between devices: 14.1 us -> none  [the longest x3 12.8 us: padded_2(): lax.ppermute(lax.slice_in_dim(block, 0, width, axis=dim), axis, backward)]
  transfers between devices with their start and end apart: 11 -> 0, of which waited for: 8 -> 0; matrix products, arithmetic and copies ran while one was open for 7% -> 0% of each run, Pallas kernels for 0% -> 0%
where the time goes in v1:
time: 74.3 us; the launch traced here: 74.1 us
  Pallas kernels  68.7 us (92%)
  local copies, waits for them, and re-layouts  2.54 us (3%)
  other arithmetic  1.51 us (2%)
  between operations  1.3 us (2%)
    pallas_call x1, Pallas kernels, on_device(): pl.pallas_call(body, out_shape=(jax.ShapeDtypeStruct((CELLS, C), BF), jax...  68.7 us
    slice x1, local copies, waits for them, and re-layouts, on_device(): return (grad_features.reshape(features.shape), scaled[1], scaled[0])  1.55 us
    mul x1, other arithmetic, on_device(): scaled = grads.astype(F32) * (1.0 / math.sqrt(8 * 128 * 256))  1.51 us

profile of v1, /device:TPU:1, one launch (start us, length us, event | category | flops | bytes accessed | tf_op | source)
XLA Modules:
  0.0 74.1 jit_solution(12591256801939804926)
XLA Ops:
  1.3 68.7 %shard_map.103 = (bf16[2048,256]{1,0:T(8,128)(2,1)}, bf16[18,256,128]{2,1,0:T(8,128)(2,1)}) custom-call(bf16[2048,256]{1,0:T(8,128)(2,1)} %bitcast.11, s32[8,256]{1,0:T(8,128)} %bitcast.15, s32[1]{0:T(128)S(6)} %copy.12.bc, f32[3,256]{1,0:T(4,128)} %scale.1, f32[8,256]{1,0:T(8,128)} %bias.1, bf16[2304,128]{1,0:T(8,128)(2,1)} %bitcast.13, ...), custom_call_target="tpu_custom_call" | custom-call | tf_op jit(solution)/shard_map/pallas_call | solution.py:430
  70.0 1.5 %convert_multiply_fusion = f32[18,256,128]{2,1,0:T(8,128)S(1)} fusion(bf16[18,256,128]{2,1,0:T(8,128)(2,1)} %get-tuple-element.6), kind=kLoop, calls=%fused_computation | loop fusion | flops 1179648 | bytes 3538944 | tf_op jit(solution)/shard_map/mul | solution.py:486
  71.5 0.0 copy-start
  71.5 1.6 %fusion = (f32[9,256,128]{2,1,0:T(8,128)}, f32[9,256,128]{2,1,0:T(8,128)}) fusion(f32[18,256,128]{2,1,0:T(8,128)S(1)} %convert_multiply_fusion), kind=kLoop, calls=%fused_computation.1 | loop fusion | bytes 4718592 | tf_op jit(solution)/shard_map/slice | solution.py:488
  73.1 0.0 copy-done
  73.1 1.0 %copy.13 = bf16[1,8,256,256]{3,2,1,0:T(8,128)(2,1)} copy(bf16[1,8,256,256]{3,2,1,0:T(8,128)(2,1)S(1)} %bitcast.10) | data formatting | bytes 2097152
Async XLA Ops:
  71.5 1.6 %copy-start = (bf16[2048,256]{1,0:T(8,128)(2,1)S(1)}, bf16[2048,256]{1,0:T(8,128)(2,1)}, u32[]{:S(2)}) copy-start(bf16[2048,256]{1,0:T(8,128)(2,1)} %get-tuple-element.5) | copy-start | bytes 3145732

commit v2 on v1

--- a/solution.py
+++ b/solution.py
@@ -17,7 +17,7 @@
 NT = (((1,), (1,)), ((), ()))
 TN = (((0,), (0,)), ((), ()))
 PIECES = 6
-LINE_AXIS = ("z", "x", "z", "x", "z", "x")
+LINE_AXIS = ("z", "y", "x", "z", "y", "x")
 SLOPE = math.sqrt(2.0 / math.pi)
 
 
@@ -33,11 +33,11 @@
 
 
 def body(
-    feat, geo, bc, scale, bias, k1, k2, cot, gf, grads,
+    feat, geo, bc, scale, bias, k1, k2, cot, gf, g_two, g_one,
     fbuf, cbuf, gbuf, geot, sbuf, bbuf, gated_halo, cot_halo, pre_halo, edge,
     xg, xc, xp, w1, w2, pre, gact, act, part,
     sib_out, sib_in, plane_out, plane_in, line_out, line_in, shard,
-    load_sem, halo_send, halo_recv, w_send, w_recv, r_send, r_recv,
+    load_sem, hop_sem, halo_send, halo_recv, w_send, w_recv, r_send, r_recv,
 ):
     dp = lax.axis_index("dp")
     sp = lax.axis_index("spatial")
@@ -54,31 +54,35 @@
     has_up, has_down = sp > 0, sp < 15
 
     def peer(axis, k):
-        side = k // 4
-        y = (cy + k % 4) % 4
+        side, step = k // 4, k % 4
         if axis == "z":
-            return (cx + side) % 4, y, dp
-        return cx, y, (dp + side) % 4
+            return (cx + side) % 4, (cy + step) % 4, dp
+        if axis == "y":
+            return (cx + side) % 4, cy, (dp + step) % 4
+        return cx, (cy + step) % 4, (dp + side) % 4
 
     barrier = pltpu.get_barrier_semaphore()
 
     def greet(target):
         pl.semaphore_signal(barrier, inc=1, device_id=target, device_id_type=MESH)
 
+    ring = []
+    for step in (1, 3):
+        ring.append(device(cx, (cy + step) % 4, dp, core))
+        ring.append(device((cx + step) % 4, cy, dp, core))
+        ring.append(device(cx, cy, (dp + step) % 4, core))
     greet(sibling)
+    for target in ring:
+        greet(target)
     pl.when(jnp.logical_and(core == 0, has_up))(lambda: greet(up))
     pl.when(jnp.logical_and(core == 1, has_down))(lambda: greet(down))
 
-    def greet_z(k, _):
-        greet(device(*peer("z", k), core))
-        return 0
-
-    def greet_x(k, _):
-        greet(device(*peer("x", k), core))
-        return 0
-
-    lax.fori_loop(1, 16, greet_z, 0)
-    lax.fori_loop(4, 16, greet_x, 0)
+    def tell(n):
+        for target in ring:
+            pl.semaphore_signal(hop_sem.at[n], inc=1, device_id=target, device_id_type=MESH)
+
+    def heard(n):
+        pl.semaphore_wait(hop_sem.at[n], 6)
 
     def load(src, dst, i):
         cp = pltpu.make_async_copy(src, dst, load_sem.at[i])
@@ -93,9 +97,6 @@
     k2_cp = load(k2, w2.at[fs], 5)
     k1_cp = load(k1, w1.at[fs], 6)
 
-    strangers = jnp.where(core == 0, jnp.where(has_up, 1, 0), jnp.where(has_down, 1, 0))
-    pl.semaphore_wait(barrier, 28 + strangers)
-
     def remote(src, dst, send, recv, target):
         return pltpu.make_async_remote_copy(
             src_ref=src, dst_ref=dst, send_sem=send, recv_sem=recv, device_id=target, device_id_type=MESH
@@ -114,8 +115,6 @@
     gated_down = halo_down(edge.at[1], 1, gated_halo)
     pre_up = halo_up(xp.at[pl.ds(WIDTH, WIDTH), pl.ds(C, C)], 2, pre_halo)
     pre_down = halo_down(xp.at[pl.ds(CELLS, WIDTH), pl.ds(C, C)], 2, pre_halo)
-    pl.when(has_up)(lambda: cot_up.start())
-    pl.when(has_down)(lambda: cot_down.start())
 
     next_a = device(cx, yh * 2 + other, dp, core)
     next_b = device(cx, (1 - yh) * 2 + other, dp, core)
@@ -131,8 +130,6 @@
 
     w1_copies = quarter_copies(0, k1, w1)
     w2_copies = quarter_copies(1, k2, w2)
-    for cp in w1_copies[:2] + w2_copies[:2]:
-        cp.start()
 
     geo_cp.wait()
     geot[...] = jnp.transpose(gbuf[...])
@@ -156,13 +153,23 @@
         return f * gain_of(row) + offset
 
     feat_cp.wait()
-    first, last = gated_row(0), gated_row(ROWS - 1)
-    edge[0] = first.astype(BF)
-    edge[1] = last.astype(BF)
+    for row in (0, 7, 1, 2, 3, 4, 5, 6):
+        value = gated_row(row)
+        put_row(xg, row + 1, value)
+        if row in (0, 7):
+            edge[row // 7] = value.astype(BF)
+
+    strangers = jnp.where(core == 0, jnp.where(has_up, 1, 0), jnp.where(has_down, 1, 0))
+    pl.semaphore_wait(barrier, 7 + strangers)
+    for cp in w1_copies[:2]:
+        cp.start()
+    pl.when(has_up)(lambda: cot_up.start())
+    pl.when(has_down)(lambda: cot_down.start())
     pl.when(has_up)(lambda: gated_up.start())
     pl.when(has_down)(lambda: gated_down.start())
-    for row in range(ROWS):
-        put_row(xg, row + 1, gated_row(row))
+    for cp in w2_copies[:2]:
+        cp.start()
+    tell(0)
 
     def put_cot(r, value):
         at = pl.ds(r * WIDTH, WIDTH)
@@ -206,6 +213,8 @@
         def _():
             put(ROWS + 1, jnp.zeros((WIDTH, C), F32))
 
+    heard(0)
+    tell(1)
     halo_rows(cot_up, cot_down, cot_halo, put_cot)
     for r in (0, 6):
         gact[r * WIDTH : (r + 2) * WIDTH, :] = grad_act_half(fs, r, 2)
@@ -216,6 +225,9 @@
     k1_cp.wait()
     w1_copies[2].wait_recv()
 
+    heard(1)
+    tell(2)
+
     def big_lhs(x, r, rows):
         return jnp.concatenate([x[pl.ds((r + d) * WIDTH, rows * WIDTH), :] for d in range(3)], axis=1)
 
@@ -231,6 +243,7 @@
         return 0
 
     lax.fori_loop(0, ROWS, act_row, 0)
+    heard(2)
 
     def sib_copy(p):
         return remote(sib_out.at[p], sib_in.at[p], r_send.at[p, 0], r_recv.at[p, 0], sibling)
@@ -246,7 +259,9 @@
         return remote(plane_in.at[p], plane_in.at[p], r_send.at[p, 1], r_recv.at[p, 1], sibling)
 
     def slot_of(x, y, z, axis):
-        return (x if axis == "z" else z) * 4 + y
+        return {"z": x * 4 + y, "y": x * 4 + z, "x": z * 4 + y}[axis]
+
+    keeps = dp % 2 == fs
 
     def stage2(p):
         axis = LINE_AXIS[p]
@@ -280,10 +295,19 @@
         line_out[p] = total.astype(BF)
 
         def send(k, _):
-            to = (cx, cy, (dp + k) % 4) if axis == "z" else ((cx + k) % 4, cy, dp)
-            remote(
-                line_out.at[p], line_in.at[p, k - 1], r_send.at[p, 2], r_recv.at[p, 2], device(*to, core)
-            ).start()
+            to = {
+                "z": (cx, cy, (dp + k) % 4), "y": (cx, (cy + k) % 4, dp), "x": ((cx + k) % 4, cy, dp)
+            }[axis]
+
+            def go():
+                remote(
+                    line_out.at[p], line_in.at[p, k - 1], r_send.at[p, 2], r_recv.at[p, 2], device(*to, core)
+                ).start()
+
+            if axis == "y":
+                pl.when((cy + k) % 2 == dp % 2)(go)
+            else:
+                go()
             return 0
 
         lax.fori_loop(1, 4, send, 0)
@@ -291,45 +315,79 @@
     def row_of(block):
         return pl.ds(pl.multiple_of(core * HALF + block * 16, 16), 16)
 
-    def gather_wait(p):
-        few = plane_in.at[p, pl.ds(0, 7)]
-        return remote(few, few, r_send.at[p, 3], r_recv.at[p, 3], sibling)
-
-    def stage4(p):
+    def line_send_wait(p):
+        def some(n):
+            return remote(line_in.at[p, pl.ds(0, n)], line_in.at[p, pl.ds(0, n)], r_send.at[p, 2], r_recv.at[p, 2], sibling)
+
+        if LINE_AXIS[p] == "y":
+            pl.when(keeps)(lambda: some(1).wait_send())
+            pl.when(jnp.logical_not(keeps))(lambda: some(2).wait_send())
+        else:
+            some(3).wait_send()
+
+    def gather_wait(p, n):
+        some = plane_in.at[p, pl.ds(0, n)]
+        return remote(some, some, r_send.at[p, 3], r_recv.at[p, 3], sibling)
+
+    def gather_recv_wait(p):
+        if LINE_AXIS[p] == "y":
+            pl.when(keeps)(lambda: gather_wait(p, 7).wait_recv())
+            pl.when(jnp.logical_not(keeps))(lambda: gather_wait(p, 8).wait_recv())
+        else:
+            gather_wait(p, 7).wait_recv()
+
+    def gather_send_wait(p):
+        if LINE_AXIS[p] == "y":
+            pl.when(keeps)(lambda: gather_wait(p, 15).wait_send())
+        else:
+            gather_wait(p, 7).wait_send()
+
+    def finish_shard(p):
         axis = LINE_AXIS[p]
         line_wait(p).wait_recv()
         total = line_out[p].astype(F32)
         for k in range(3):
             total = total + line_in[p, k].astype(F32)
         shard[p] = total.astype(BF)
-        block = (cx if axis == "z" else dp) * 2 + yh
-        grads[3 * p : 3 * p + 3, row_of(block), :] = total.astype(BF)
+        block = {"z": cx * 2 + yh, "y": cx * 2 + dp // 2, "x": dp * 2 + yh}[axis]
+        three = pl.ds(3 * (p % 3), 3)
+        grads = (g_two, g_one)[p // 3]
+        grads[three, row_of(block), :] = total.astype(BF)
 
         def send(k, _):
             y = ((yh + k) % 2) * 2 + fs
-            to = ((cx + k // 2) % 4, y, dp) if axis == "z" else (cx, y, (dp + k // 2) % 4)
+            if axis == "z":
+                to = (cx + k // 2) % 4, y, dp
+            elif axis == "y":
+                to = peer("y", k)
+            else:
+                to = cx, y, (dp + k // 2) % 4
             remote(
-                shard.at[p], grads.at[pl.ds(3 * p, 3), row_of(block)],
+                shard.at[p], grads.at[three, row_of(block)],
                 r_send.at[p, 3], r_recv.at[p, 3], device(*to, core),
             ).start()
             return 0
 
-        lax.fori_loop(1, 8, send, 0)
+        lax.fori_loop(1, 16 if axis == "y" else 8, send, 0)
+
+    def stage4(p):
+        if LINE_AXIS[p] == "y":
+            pl.when(keeps)(lambda: finish_shard(p))
+        else:
+            finish_shard(p)
 
     def last_copy(p):
-        at = grads.at[pl.ds(3 * p, 3), pl.ds(pl.multiple_of(core * HALF, HALF), HALF)]
+        at = (g_two, g_one)[p // 3].at[pl.ds(3 * (p % 3), 3), pl.ds(pl.multiple_of(core * HALF, HALF), HALF)]
         return remote(at, at, r_send.at[p, 4], r_recv.at[p, 4], sibling)
 
     def stage5(p):
-        gather_wait(p).wait_recv()
+        gather_recv_wait(p)
         last_copy(p).start()
 
     for d in range(3):
         for e in range(3):
-            for h in range(2):
-                part[d, e, :, h * HALF : (h + 1) * HALF] = dot(
-                    act[...], xc[h, pl.ds((2 - d) * WIDTH, CELLS), (2 - e) * HALF : (3 - e) * HALF], TN
-                )
+            at, lanes = pl.ds((2 - d) * WIDTH, CELLS), slice((2 - e) * HALF, (3 - e) * HALF)
+            part[d, e] = dot(act[...], jnp.concatenate([xc[0, at, lanes], xc[1, at, lanes]], axis=1), TN)
         stage1(d)
         if d >= 1:
             stage2(d - 1)
@@ -412,8 +470,8 @@
     for p in range(PIECES):
         sib_copy(p).wait_send()
         plane_wait(p).wait_send()
-        line_wait(p).wait_send()
-        gather_wait(p).wait_send()
+        line_send_wait(p)
+        gather_send_wait(p)
         last_copy(p).wait_send()
     for cp in w1_copies + w2_copies:
         cp.wait_send()
@@ -427,14 +485,15 @@
     any_spec = pl.BlockSpec(memory_space=pl.ANY)
     vmem = pltpu.VMEM
     dma = pltpu.SemaphoreType.DMA
-    grad_features, grads = pl.pallas_call(
+    grad_features, g_two, g_one = pl.pallas_call(
         body,
         out_shape=(
             jax.ShapeDtypeStruct((CELLS, C), BF),
-            jax.ShapeDtypeStruct((18, C, HALF), BF),
+            jax.ShapeDtypeStruct((9, C, HALF), BF),
+            jax.ShapeDtypeStruct((9, C, HALF), BF),
         ),
         in_specs=[any_spec, any_spec, pl.BlockSpec(memory_space=pltpu.SMEM)] + [any_spec] * 5,
-        out_specs=(any_spec, pl.BlockSpec(memory_space=pltpu.VMEM)),
+        out_specs=(any_spec, pl.BlockSpec(memory_space=pltpu.VMEM), pl.BlockSpec(memory_space=pltpu.VMEM)),
         scratch_shapes=[
             vmem((CELLS, C), BF),
             vmem((CELLS, C), BF),
@@ -463,6 +522,7 @@
             vmem((PIECES, 3, 3, 16, HALF), BF),
             vmem((PIECES, 3, 16, HALF), BF),
             dma((7,)),
+            pltpu.SemaphoreType.REGULAR((3,)),
             dma((3, 2)),
             dma((3, 2)),
             dma((2, 3)),
@@ -483,9 +543,12 @@
         kernel_two.reshape(9 * C, HALF),
         cotangent.reshape(CELLS, C),
     )
-    scaled = grads.astype(F32) * (1.0 / math.sqrt(8 * 128 * 256))
-    scaled = scaled.reshape(2, 3, 3, C, HALF)
-    return grad_features.reshape(features.shape), scaled[1], scaled[0]
+    factor = 1.0 / math.sqrt(8 * 128 * 256)
+
+    def scaled(g):
+        return (g.astype(F32) * factor).reshape(3, 3, C, HALF)
+
+    return grad_features.reshape(features.shape), scaled(g_one), scaled(g_two)
 
 
 def solution(mesh):

time: 74.3 us -> 69.2 us (0.931)
  Pallas kernels: 68.7 us -> 63.8 us
  local copies, waits for them, and re-layouts: 2.54 us -> 0.97 us
  other arithmetic: 1.51 us -> 2.98 us
    pallas_call x1, Pallas kernels: 68.7 us -> 63.8 us  [on_device(): pl.pallas_call(body, out_shape=(jax.ShapeDtypeStruct((CELLS, C), BF), jax...]
    slice x1 -> x0, local copies, waits for them, and re-layouts: 1.55 us -> none  [on_device(): return (grad_features.reshape(features.shape), scaled[1], scaled[0])]
    mul x1, other arithmetic: 1.51 us -> 2.98 us  [scaled(): return (g.astype(F32) * factor).reshape(3, 3, C, HALF)]
where the time goes in v2:
time: 69.2 us; the launch traced here: 69 us
  Pallas kernels  63.8 us (92%)
  other arithmetic  2.98 us (4%)
  between operations  1.3 us (2%)
  local copies, waits for them, and re-layouts  0.97 us (1%)
    pallas_call x1, Pallas kernels, on_device(): pl.pallas_call(body, out_shape=(jax.ShapeDtypeStruct((CELLS, C), BF), jax...  63.8 us
    mul x1, other arithmetic, scaled(): return (g.astype(F32) * factor).reshape(3, 3, C, HALF)  2.98 us

profile of v2, /device:TPU:1, one launch (start us, length us, event | category | flops | bytes accessed | tf_op | source)
XLA Modules:
  0.0 69.0 jit_solution(16844259866417371967)
XLA Ops:
  1.3 63.8 %shard_map.103 = (bf16[2048,256]{1,0:T(8,128)(2,1)}, bf16[9,256,128]{2,1,0:T(8,128)(2,1)}, bf16[9,256,128]{2,1,0:T(8,128)(2,1)}) custom-call(bf16[2048,256]{1,0:T(8,128)(2,1)} %bitcast.11, s32[8,256]{1,0:T(8,128)} %bitcast.15, s32[1]{0:T(128)S(6)} %copy.12.bc, f32[3,256]{1,0:T(4,128)} %scale.1, f32[8,256]{1,0:T(8,128)} %bias.1, bf16[2304,128]{1,0:T(8,128)(2,1)} %bitcast.13, ...), custom_call_target="tpu_custom_call" | custom-call | tf_op jit(solution)/shard_map/pallas_call | solution.py:488
  65.1 0.0 copy-start
  65.1 3.0 %convert_multiply_fusion = (f32[9,256,128]{2,1,0:T(8,128)}, f32[9,256,128]{2,1,0:T(8,128)}) fusion(bf16[9,256,128]{2,1,0:T(8,128)(2,1)} %get-tuple-element.8, bf16[9,256,128]{2,1,0:T(8,128)(2,1)} %get-tuple-element.7), kind=kLoop, calls=%fused_computation | loop fusion | flops 1179648 | bytes 3538944 | tf_op jit(solution)/shard_map/mul | solution.py:549
  68.1 0.0 copy-done
  68.1 1.0 %copy.13 = bf16[1,8,256,256]{3,2,1,0:T(8,128)(2,1)} copy(bf16[1,8,256,256]{3,2,1,0:T(8,128)(2,1)S(1)} %bitcast.10) | data formatting | bytes 2097152
Async XLA Ops:
  65.1 3.0 %copy-start = (bf16[2048,256]{1,0:T(8,128)(2,1)S(1)}, bf16[2048,256]{1,0:T(8,128)(2,1)}, u32[]{:S(2)}) copy-start(bf16[2048,256]{1,0:T(8,128)(2,1)} %get-tuple-element.6) | copy-start | bytes 3145732

commit v3 on v2

--- a/solution.py
+++ b/solution.py
@@ -15,7 +15,6 @@
 QUARTER = 9 * C // 4
 NN = (((1,), (0,)), ((), ()))
 NT = (((1,), (1,)), ((), ()))
-TN = (((0,), (0,)), ((), ()))
 PIECES = 6
 LINE_AXIS = ("z", "y", "x", "z", "y", "x")
 SLOPE = math.sqrt(2.0 / math.pi)
@@ -34,8 +33,8 @@
 
 def body(
     feat, geo, bc, scale, bias, k1, k2, cot, gf, g_two, g_one,
-    fbuf, cbuf, gbuf, geot, sbuf, bbuf, gated_halo, cot_halo, pre_halo, edge,
-    xg, xc, xp, w1, w2, pre, gact, act, part,
+    code, fbuf, cbuf, gbuf, geot, sbuf, bbuf, gated_halo, cot_halo, pre_halo, edge,
+    xg, xgt, xc, xp, w1, w2, slope, gact, actt, part,
     sib_out, sib_in, plane_out, plane_in, line_out, line_in, shard,
     load_sem, hop_sem, halo_send, halo_recv, w_send, w_recv, r_send, r_recv,
 ):
@@ -46,20 +45,22 @@
     cy = yh * 2 + fs
     other = 1 - fs
 
-    def device(x, y, z, c):
-        return (z, ((y // 2) * 4 + x) * 2 + c, y % 2)
-
-    sibling = device(cx, cy, dp, 1 - core)
+    xs = [cx] + [(cx + i) % 4 for i in range(1, 4)]
+    ys = [cy] + [(cy + i) % 4 for i in range(1, 4)]
+    zs = [dp] + [(dp + i) % 4 for i in range(1, 4)]
+    y_part = [(y // 2) * 8 + core for y in ys]
+    y_fs = [y % 2 for y in ys]
+
+    def device(i, j, k):
+        return (zs[k], y_part[j] + 2 * xs[i], y_fs[j])
+
+    sibling = (dp, sp + 1 - 2 * core, fs)
     up, down = (dp, sp - 1, fs), (dp, sp + 1, fs)
     has_up, has_down = sp > 0, sp < 15
 
-    def peer(axis, k):
+    def offset_of(axis, k):
         side, step = k // 4, k % 4
-        if axis == "z":
-            return (cx + side) % 4, (cy + step) % 4, dp
-        if axis == "y":
-            return (cx + side) % 4, cy, (dp + step) % 4
-        return cx, (cy + step) % 4, (dp + side) % 4
+        return {"z": (side, step, 0), "y": (side, 0, step), "x": (0, step, side)}[axis]
 
     barrier = pltpu.get_barrier_semaphore()
 
@@ -68,9 +69,7 @@
 
     ring = []
     for step in (1, 3):
-        ring.append(device(cx, (cy + step) % 4, dp, core))
-        ring.append(device((cx + step) % 4, cy, dp, core))
-        ring.append(device(cx, cy, (dp + step) % 4, core))
+        ring += [device(0, step, 0), device(step, 0, 0), device(0, 0, step)]
     greet(sibling)
     for target in ring:
         greet(target)
@@ -89,6 +88,7 @@
         cp.start()
         return cp
 
+    bc_cp = load(bc, code, 7)
     geo_cp = load(geo, gbuf, 0)
     scale_cp = load(scale, sbuf, 1)
     bias_cp = load(bias, bbuf, 2)
@@ -116,8 +116,8 @@
     pre_up = halo_up(xp.at[pl.ds(WIDTH, WIDTH), pl.ds(C, C)], 2, pre_halo)
     pre_down = halo_down(xp.at[pl.ds(CELLS, WIDTH), pl.ds(C, C)], 2, pre_halo)
 
-    next_a = device(cx, yh * 2 + other, dp, core)
-    next_b = device(cx, (1 - yh) * 2 + other, dp, core)
+    next_a = (dp, sp, other)
+    next_b = (dp, (1 - yh) * 8 + cx * 2 + core, other)
 
     def quarter_copies(i, src, w):
         out = []
@@ -135,13 +135,14 @@
     geot[...] = jnp.transpose(gbuf[...])
     scale_cp.wait()
     bias_cp.wait()
+    bc_cp.wait()
     classes = lax.broadcasted_iota(jnp.int32, (8, C), 0)
-    offset = jnp.sum(jnp.where(classes == bc[0], bbuf[...], 0.0), axis=0, keepdims=True)
+    offset = jnp.sum(jnp.where(classes == code[0], bbuf[...], 0.0), axis=0, keepdims=True)
 
     def gain_of(row):
-        code = geot[:, row : row + 1]
+        cell = geot[:, row : row + 1]
         return jnp.where(
-            code == 0, sbuf[0:1, :], jnp.where(code == 1, sbuf[1:2, :], sbuf[2:3, :])
+            cell == 0, sbuf[0:1, :], jnp.where(cell == 1, sbuf[1:2, :], sbuf[2:3, :])
         )
 
     def put_row(x, r, value):
@@ -218,10 +219,20 @@
     halo_rows(cot_up, cot_down, cot_halo, put_cot)
     for r in (0, 6):
         gact[r * WIDTH : (r + 2) * WIDTH, :] = grad_act_half(fs, r, 2)
+
+    def turn(r):
+        at = pl.ds(r * WIDTH, WIDTH)
+        for e in range(3):
+            xgt[e * C : (e + 1) * C, at] = jnp.transpose(xg[at, e * C : (e + 1) * C])
+
+    for r in range(1, ROWS + 1):
+        turn(r)
     for cp in w1_copies[:2]:
         cp.wait_recv()
     w1_copies[2].start()
     halo_rows(gated_up, gated_down, gated_halo, functools.partial(put_row, xg))
+    turn(0)
+    turn(ROWS + 1)
     k1_cp.wait()
     w1_copies[2].wait_recv()
 
@@ -231,18 +242,20 @@
     def big_lhs(x, r, rows):
         return jnp.concatenate([x[pl.ds((r + d) * WIDTH, rows * WIDTH), :] for d in range(3)], axis=1)
 
-    pre[...] = dot(big_lhs(xg, 0, ROWS), jnp.concatenate([w1[0], w1[1]], axis=1), NN)
+    def act_rows(r):
+        v = dot(big_lhs(xg, r, 2), jnp.concatenate([w1[0], w1[1]], axis=1), NN)
+        at = slice(r * WIDTH, (r + 2) * WIDTH)
+        sq = v * v
+        t = jnp.tanh(SLOPE * (v + 0.044715 * (sq * v)))
+        half = 0.5 * (1.0 + t)
+        slope[at, :] = half + 0.5 * v * (1.0 - t * t) * (SLOPE * (1.0 + (3 * 0.044715) * sq))
+        actt[:, at] = jnp.transpose((v * half).astype(BF))
+
+    for r in (0, 2, 4, 6):
+        act_rows(r)
     for cp in w2_copies[:2]:
         cp.wait_recv()
     w2_copies[2].start()
-
-    def act_row(row, _):
-        at = pl.ds(pl.multiple_of(row * WIDTH, WIDTH), WIDTH)
-        v = pre[at, :]
-        act[at, :] = (0.5 * v * (1.0 + jnp.tanh(SLOPE * (v + 0.044715 * (v * v * v))))).astype(BF)
-        return 0
-
-    lax.fori_loop(0, ROWS, act_row, 0)
     heard(2)
 
     def sib_copy(p):
@@ -258,7 +271,8 @@
     def plane_wait(p):
         return remote(plane_in.at[p], plane_in.at[p], r_send.at[p, 1], r_recv.at[p, 1], sibling)
 
-    def slot_of(x, y, z, axis):
+    def slot_of(i, j, k, axis):
+        x, y, z = xs[i], ys[j], zs[k]
         return {"z": x * 4 + y, "y": x * 4 + z, "x": z * 4 + y}[axis]
 
     keeps = dp % 2 == fs
@@ -273,15 +287,12 @@
                     :, block * 16 : (block + 1) * 16, h * HALF : (h + 1) * HALF
                 ].astype(BF)
 
-        def send(k, _):
-            to = peer(axis, k)
+        for k in range(1, 16):
+            to = offset_of(axis, k)
             remote(
                 plane_out.at[p, slot_of(*to, axis)], plane_in.at[p, k - 1],
-                r_send.at[p, 1], r_recv.at[p, 1], device(*to, core),
+                r_send.at[p, 1], r_recv.at[p, 1], device(*to),
             ).start()
-            return 0
-
-        lax.fori_loop(1, 16, send, 0)
 
     def line_wait(p):
         return remote(line_in.at[p], line_in.at[p], r_send.at[p, 2], r_recv.at[p, 2], sibling)
@@ -289,28 +300,21 @@
     def stage3(p):
         axis = LINE_AXIS[p]
         plane_wait(p).wait_recv()
-        total = plane_out[p, slot_of(cx, cy, dp, axis)].astype(F32)
+        total = plane_out[p, slot_of(0, 0, 0, axis)].astype(F32)
         for k in range(15):
             total = total + plane_in[p, k].astype(F32)
         line_out[p] = total.astype(BF)
 
-        def send(k, _):
-            to = {
-                "z": (cx, cy, (dp + k) % 4), "y": (cx, (cy + k) % 4, dp), "x": ((cx + k) % 4, cy, dp)
-            }[axis]
-
-            def go():
-                remote(
-                    line_out.at[p], line_in.at[p, k - 1], r_send.at[p, 2], r_recv.at[p, 2], device(*to, core)
-                ).start()
+        for k in range(1, 4):
+            to = {"z": (0, 0, k), "y": (0, k, 0), "x": (k, 0, 0)}[axis]
+
+            def go(k=k, to=to):
+                remote(line_out.at[p], line_in.at[p, k - 1], r_send.at[p, 2], r_recv.at[p, 2], device(*to)).start()
 
             if axis == "y":
-                pl.when((cy + k) % 2 == dp % 2)(go)
+                pl.when(y_fs[k] == dp % 2)(go)
             else:
                 go()
-            return 0
-
-        lax.fori_loop(1, 4, send, 0)
 
     def row_of(block):
         return pl.ds(pl.multiple_of(core * HALF + block * 16, 16), 16)
@@ -354,21 +358,13 @@
         grads = (g_two, g_one)[p // 3]
         grads[three, row_of(block), :] = total.astype(BF)
 
-        def send(k, _):
-            y = ((yh + k) % 2) * 2 + fs
-            if axis == "z":
-                to = (cx + k // 2) % 4, y, dp
-            elif axis == "y":
-                to = peer("y", k)
-            else:
-                to = cx, y, (dp + k // 2) % 4
+        for k in range(1, 16):
+            to = offset_of(axis, k)
+            if axis != "y" and to[1] % 2:
+                continue
             remote(
-                shard.at[p], grads.at[three, row_of(block)],
-                r_send.at[p, 3], r_recv.at[p, 3], device(*to, core),
+                shard.at[p], grads.at[three, row_of(block)], r_send.at[p, 3], r_recv.at[p, 3], device(*to)
             ).start()
-            return 0
-
-        lax.fori_loop(1, 16 if axis == "y" else 8, send, 0)
 
     def stage4(p):
         if LINE_AXIS[p] == "y":
@@ -387,7 +383,7 @@
     for d in range(3):
         for e in range(3):
             at, lanes = pl.ds((2 - d) * WIDTH, CELLS), slice((2 - e) * HALF, (3 - e) * HALF)
-            part[d, e] = dot(act[...], jnp.concatenate([xc[0, at, lanes], xc[1, at, lanes]], axis=1), TN)
+            part[d, e] = dot(actt[...], jnp.concatenate([xc[0, at, lanes], xc[1, at, lanes]], axis=1), NN)
         stage1(d)
         if d >= 1:
             stage2(d - 1)
@@ -396,12 +392,7 @@
 
     def grad_pre_rows(r):
         at = slice(r * WIDTH, (r + 2) * WIDTH)
-        g = gact[at, :] + grad_act_half(other, r, 2)
-        v = pre[at, :]
-        sq = v * v
-        t = jnp.tanh(SLOPE * (v + 0.044715 * (sq * v)))
-        slope = 0.5 * (1.0 + t) + 0.5 * v * (1.0 - t * t) * (SLOPE * (1.0 + (3 * 0.044715) * sq))
-        g = g * slope
+        g = (gact[at, :] + grad_act_half(other, r, 2)) * slope[at, :]
         for i in range(2):
             put_row(xp, r + i + 1, g[i * WIDTH : (i + 1) * WIDTH])
 
@@ -411,27 +402,19 @@
     pl.when(has_down)(lambda: pre_down.start())
     stage2(2)
     grad_pre_rows(2)
-    stage3(0)
     grad_pre_rows(4)
-    stage3(1)
 
     for d in range(3):
         p = 3 + d
+        three = dot(xgt[:, pl.ds(d * WIDTH, CELLS)], xp[pl.ds(WIDTH, CELLS), C : 2 * C], NN)
         for e in range(3):
-            part[p, e] = dot(
-                xg[pl.ds(d * WIDTH, CELLS), e * C : (e + 1) * C], xp[pl.ds(WIDTH, CELLS), C : 2 * C], TN
-            )
+            part[p, e] = three[e * C : (e + 1) * C]
         stage1(p)
-        if d == 0:
-            stage3(2)
-            stage4(0)
-        elif d == 1:
+        if d == 1:
             stage2(3)
-            stage4(1)
-        else:
+        elif d == 2:
             stage2(4)
-            stage4(2)
-            stage5(0)
+            stage3(0)
 
     halo_rows(pre_up, pre_down, pre_halo, functools.partial(put_row, xp))
 
@@ -448,16 +431,22 @@
 
     back_rows(0)
     stage2(5)
+    stage3(1)
+    back_rows(2)
+    stage3(2)
+    back_rows(4)
+    stage4(0)
     stage3(3)
-    back_rows(2)
-    stage3(4)
-    stage5(1)
-    back_rows(4)
-    stage3(5)
-    stage4(3)
     back_rows(6)
     out_cp = pltpu.make_async_copy(fbuf, gf, load_sem.at[3])
     out_cp.start()
+    stage4(1)
+    stage3(4)
+    stage4(2)
+    stage3(5)
+    stage5(0)
+    stage4(3)
+    stage5(1)
     stage4(4)
     stage5(2)
     stage4(5)
@@ -492,9 +481,10 @@
             jax.ShapeDtypeStruct((9, C, HALF), BF),
             jax.ShapeDtypeStruct((9, C, HALF), BF),
         ),
-        in_specs=[any_spec, any_spec, pl.BlockSpec(memory_space=pltpu.SMEM)] + [any_spec] * 5,
+        in_specs=[any_spec] * 8,
         out_specs=(any_spec, pl.BlockSpec(memory_space=pltpu.VMEM), pl.BlockSpec(memory_space=pltpu.VMEM)),
         scratch_shapes=[
+            pltpu.SMEM((1,), jnp.int32),
             vmem((CELLS, C), BF),
             vmem((CELLS, C), BF),
             vmem((ROWS, WIDTH), jnp.int32),
@@ -506,13 +496,14 @@
             vmem((2, WIDTH, C), BF),
             vmem((2, WIDTH, C), BF),
             vmem((CELLS + 2 * WIDTH, 3 * C), BF),
+            vmem((3 * C, CELLS + 2 * WIDTH), BF),
             vmem((2, CELLS + 2 * WIDTH, 3 * HALF), BF),
             vmem((CELLS + 2 * WIDTH, 3 * C), BF),
             vmem((2, 9 * C, HALF), BF),
             vmem((2, 9 * C, HALF), BF),
             vmem((CELLS, C), F32),
             vmem((CELLS, C), F32),
-            vmem((CELLS, C), BF),
+            vmem((C, CELLS), BF),
             vmem((PIECES, 3, C, C), F32),
             vmem((PIECES, 3, HALF, C), BF),
             vmem((PIECES, 3, HALF, C), BF),
@@ -521,7 +512,7 @@
             vmem((PIECES, 3, 16, HALF), BF),
             vmem((PIECES, 3, 3, 16, HALF), BF),
             vmem((PIECES, 3, 16, HALF), BF),
-            dma((7,)),
+            dma((8,)),
             pltpu.SemaphoreType.REGULAR((3,)),
             dma((3, 2)),
             dma((3, 2)),

time: 69.2 us -> 61.7 us (0.89)
  Pallas kernels: 63.8 us -> 56.3 us
    pallas_call x1, Pallas kernels: 63.8 us -> 56.3 us  [on_device(): pl.pallas_call(body, out_shape=(jax.ShapeDtypeStruct((CELLS, C), BF), jax...]
where the time goes in v3:
time: 61.7 us; the launch traced here: 61.5 us
  Pallas kernels  56.3 us (91%)
  other arithmetic  2.98 us (5%)
  between operations  1.3 us (2%)
  local copies, waits for them, and re-layouts  0.97 us (2%)
    pallas_call x1, Pallas kernels, on_device(): pl.pallas_call(body, out_shape=(jax.ShapeDtypeStruct((CELLS, C), BF), jax...  56.3 us
    mul x1, other arithmetic, scaled(): return (g.astype(F32) * factor).reshape(3, 3, C, HALF)  2.98 us

profile of v3, /device:TPU:1, one launch (start us, length us, event | category | flops | bytes accessed | tf_op | source)
XLA Modules:
  0.0 61.5 jit_solution(6269074955700018310)
XLA Ops:
  1.3 56.3 %shard_map.103 = (bf16[2048,256]{1,0:T(8,128)(2,1)}, bf16[9,256,128]{2,1,0:T(8,128)(2,1)}, bf16[9,256,128]{2,1,0:T(8,128)(2,1)}) custom-call(bf16[2048,256]{1,0:T(8,128)(2,1)} %bitcast.11, s32[8,256]{1,0:T(8,128)} %bitcast.15, s32[1]{0:T(128)S(6)} %copy.12.bc, f32[3,256]{1,0:T(4,128)} %scale.1, f32[8,256]{1,0:T(8,128)} %bias.1, bf16[2304,128]{1,0:T(8,128)(2,1)} %bitcast.13, ...), custom_call_target="tpu_custom_call" | custom-call | tf_op jit(solution)/shard_map/pallas_call | solution.py:477
  57.5 0.0 copy-start
  57.6 3.0 %convert_multiply_fusion = (f32[9,256,128]{2,1,0:T(8,128)}, f32[9,256,128]{2,1,0:T(8,128)}) fusion(bf16[9,256,128]{2,1,0:T(8,128)(2,1)} %get-tuple-element.8, bf16[9,256,128]{2,1,0:T(8,128)(2,1)} %get-tuple-element.7), kind=kLoop, calls=%fused_computation | loop fusion | flops 1179648 | bytes 3538944 | tf_op jit(solution)/shard_map/mul | solution.py:540
  60.5 0.0 copy-done
  60.5 1.0 %copy.13 = bf16[1,8,256,256]{3,2,1,0:T(8,128)(2,1)} copy(bf16[1,8,256,256]{3,2,1,0:T(8,128)(2,1)S(1)} %bitcast.10) | data formatting | bytes 2097152
Async XLA Ops:
  57.5 3.0 %copy-start = (bf16[2048,256]{1,0:T(8,128)(2,1)S(1)}, bf16[2048,256]{1,0:T(8,128)(2,1)}, u32[]{:S(2)}) copy-start(bf16[2048,256]{1,0:T(8,128)(2,1)} %get-tuple-element.6) | copy-start | bytes 3145732

commit v4 on v3

--- a/solution.py
+++ b/solution.py
@@ -16,6 +16,7 @@
 NN = (((1,), (0,)), ((), ()))
 NT = (((1,), (1,)), ((), ()))
 PIECES = 6
+LAST = 5
 LINE_AXIS = ("z", "y", "x", "z", "y", "x")
 SLOPE = math.sqrt(2.0 / math.pi)
 
@@ -35,7 +36,7 @@
     feat, geo, bc, scale, bias, k1, k2, cot, gf, g_two, g_one,
     code, fbuf, cbuf, gbuf, geot, sbuf, bbuf, gated_halo, cot_halo, pre_halo, edge,
     xg, xgt, xc, xp, w1, w2, slope, gact, actt, part,
-    sib_out, sib_in, plane_out, plane_in, line_out, line_in, shard,
+    sib_out, sib_in, plane_out, plane_in, line_out, line_in, shard, gather_in,
     load_sem, hop_sem, halo_send, halo_recv, w_send, w_recv, r_send, r_recv,
 ):
     dp = lax.axis_index("dp")
@@ -53,6 +54,9 @@
 
     def device(i, j, k):
         return (zs[k], y_part[j] + 2 * xs[i], y_fs[j])
+
+    def across(i, j, k):
+        return (zs[k], y_part[j] + 2 * xs[i] + 1 - 2 * core, y_fs[j])
 
     sibling = (dp, sp + 1 - 2 * core, fs)
     up, down = (dp, sp - 1, fs), (dp, sp + 1, fs)
@@ -214,12 +218,6 @@
         def _():
             put(ROWS + 1, jnp.zeros((WIDTH, C), F32))
 
-    heard(0)
-    tell(1)
-    halo_rows(cot_up, cot_down, cot_halo, put_cot)
-    for r in (0, 6):
-        gact[r * WIDTH : (r + 2) * WIDTH, :] = grad_act_half(fs, r, 2)
-
     def turn(r):
         at = pl.ds(r * WIDTH, WIDTH)
         for e in range(3):
@@ -227,9 +225,15 @@
 
     for r in range(1, ROWS + 1):
         turn(r)
+    heard(0)
+    tell(1)
     for cp in w1_copies[:2]:
         cp.wait_recv()
     w1_copies[2].start()
+    halo_rows(cot_up, cot_down, cot_halo, put_cot)
+    for r in (0, 6):
+        gact[r * WIDTH : (r + 2) * WIDTH, :] = grad_act_half(fs, r, 2)
+
     halo_rows(gated_up, gated_down, gated_halo, functools.partial(put_row, xg))
     turn(0)
     turn(ROWS + 1)
@@ -257,6 +261,7 @@
         cp.wait_recv()
     w2_copies[2].start()
     heard(2)
+    tell(3)
 
     def sib_copy(p):
         return remote(sib_out.at[p], sib_in.at[p], r_send.at[p, 0], r_recv.at[p, 0], sibling)
@@ -316,9 +321,6 @@
             else:
                 go()
 
-    def row_of(block):
-        return pl.ds(pl.multiple_of(core * HALF + block * 16, 16), 16)
-
     def line_send_wait(p):
         def some(n):
             return remote(line_in.at[p, pl.ds(0, n)], line_in.at[p, pl.ds(0, n)], r_send.at[p, 2], r_recv.at[p, 2], sibling)
@@ -330,7 +332,7 @@
             some(3).wait_send()
 
     def gather_wait(p, n):
-        some = plane_in.at[p, pl.ds(0, n)]
+        some = gather_in.at[p, pl.ds(0, n)]
         return remote(some, some, r_send.at[p, 3], r_recv.at[p, 3], sibling)
 
     def gather_recv_wait(p):
@@ -338,13 +340,25 @@
             pl.when(keeps)(lambda: gather_wait(p, 7).wait_recv())
             pl.when(jnp.logical_not(keeps))(lambda: gather_wait(p, 8).wait_recv())
         else:
-            gather_wait(p, 7).wait_recv()
+            gather_wait(p, 15 if p == LAST else 7).wait_recv()
 
     def gather_send_wait(p):
         if LINE_AXIS[p] == "y":
             pl.when(keeps)(lambda: gather_wait(p, 15).wait_send())
         else:
-            gather_wait(p, 7).wait_send()
+            gather_wait(p, 15 if p == LAST else 7).wait_send()
+
+    def gather_list(p):
+        offsets = [offset_of(LINE_AXIS[p], k) for k in range(16)]
+        if LINE_AXIS[p] != "y":
+            offsets = [to for to in offsets if to[1] % 2 == 0]
+        return [(to, True) for to in offsets[1:]] + [(to, False) for to in offsets if p == LAST]
+
+    def place(p, value, to, c):
+        x, y, z = (of[(4 - step) % 4] for of, step in zip((xs, ys, zs), to, strict=True))
+        block = {"z": x * 2 + y // 2, "y": x * 2 + z // 2, "x": z * 2 + y // 2}[LINE_AXIS[p]]
+        grads, three = (g_two, g_one)[p // 3], pl.ds(3 * (p % 3), 3)
+        grads[three, pl.ds(pl.multiple_of(c * HALF + block * 16, 16), 16), :] = value
 
     def finish_shard(p):
         axis = LINE_AXIS[p]
@@ -353,17 +367,10 @@
         for k in range(3):
             total = total + line_in[p, k].astype(F32)
         shard[p] = total.astype(BF)
-        block = {"z": cx * 2 + yh, "y": cx * 2 + dp // 2, "x": dp * 2 + yh}[axis]
-        three = pl.ds(3 * (p % 3), 3)
-        grads = (g_two, g_one)[p // 3]
-        grads[three, row_of(block), :] = total.astype(BF)
-
-        for k in range(1, 16):
-            to = offset_of(axis, k)
-            if axis != "y" and to[1] % 2:
-                continue
+        place(p, total.astype(BF), (0, 0, 0), core)
+        for slot, (to, same) in enumerate(gather_list(p)):
             remote(
-                shard.at[p], grads.at[three, row_of(block)], r_send.at[p, 3], r_recv.at[p, 3], device(*to)
+                shard.at[p], gather_in.at[p, slot], r_send.at[p, 3], r_recv.at[p, 3], device(*to) if same else across(*to)
             ).start()
 
     def stage4(p):
@@ -378,7 +385,17 @@
 
     def stage5(p):
         gather_recv_wait(p)
-        last_copy(p).start()
+        for slot, (to, same) in enumerate(gather_list(p)):
+
+            def put(slot=slot, to=to, same=same):
+                place(p, gather_in[p, slot], to, core if same else 1 - core)
+
+            if LINE_AXIS[p] == "y":
+                pl.when(zs[(4 - to[2]) % 4] % 2 == fs)(put)
+            else:
+                put()
+        if p != LAST:
+            last_copy(p).start()
 
     for d in range(3):
         for e in range(3):
@@ -388,6 +405,7 @@
         if d >= 1:
             stage2(d - 1)
 
+    heard(3)
     w2_copies[2].wait_recv()
 
     def grad_pre_rows(r):
@@ -453,7 +471,7 @@
     stage5(3)
     stage5(4)
     stage5(5)
-    for p in range(PIECES):
+    for p in range(LAST):
         last_copy(p).wait_recv()
 
     for p in range(PIECES):
@@ -461,13 +479,40 @@
         plane_wait(p).wait_send()
         line_send_wait(p)
         gather_send_wait(p)
-        last_copy(p).wait_send()
+        if p != LAST:
+            last_copy(p).wait_send()
     for cp in w1_copies + w2_copies:
         cp.wait_send()
     for ups, downs in ((cot_up, cot_down), (gated_up, gated_down), (pre_up, pre_down)):
         pl.when(has_up)(lambda ups=ups: ups.wait_send())
         pl.when(has_down)(lambda downs=downs: downs.wait_send())
     out_cp.wait()
+
+
+def finish(gf, g_two, g_one, gf_out, two_out, one_out, raw, wide, held, sem):
+    factor = 1.0 / math.sqrt(8 * 128 * 256)
+    loads, stores = [], []
+    for n in range(6):
+        src, dst = ((g_two, two_out), (g_one, one_out))[n // 3]
+        at = pl.ds(3 * (n % 3), 3)
+        loads.append(pltpu.make_async_copy(src.at[at], raw.at[n], sem.at[n]))
+        stores.append(pltpu.make_async_copy(wide.at[n], dst.at[at], sem.at[6 + n]))
+    for cp in loads:
+        cp.start()
+    halves = [pl.ds(n * CELLS // 2, CELLS // 2) for n in range(2)]
+    ins = [pltpu.make_async_copy(gf.at[at], held.at[at], sem.at[12 + n]) for n, at in enumerate(halves)]
+    outs = [pltpu.make_async_copy(held.at[at], gf_out.at[at], sem.at[14 + n]) for n, at in enumerate(halves)]
+    for cp in ins:
+        cp.start()
+    for n in range(6):
+        loads[n].wait()
+        wide[n] = raw[n].astype(F32) * factor
+        stores[n].start()
+        if n in (2, 5):
+            ins[n // 3].wait()
+            outs[n // 3].start()
+    for cp in stores + outs:
+        cp.wait()
 
 
 def on_device(features, geometry, bc_class, code_scale, bc_bias, kernel_one, kernel_two, cotangent):
@@ -512,8 +557,9 @@
             vmem((PIECES, 3, 16, HALF), BF),
             vmem((PIECES, 3, 3, 16, HALF), BF),
             vmem((PIECES, 3, 16, HALF), BF),
+            vmem((PIECES, 15, 3, 16, HALF), BF),
             dma((8,)),
-            pltpu.SemaphoreType.REGULAR((3,)),
+            pltpu.SemaphoreType.REGULAR((4,)),
             dma((3, 2)),
             dma((3, 2)),
             dma((2, 3)),
@@ -534,12 +580,20 @@
         kernel_two.reshape(9 * C, HALF),
         cotangent.reshape(CELLS, C),
     )
-    factor = 1.0 / math.sqrt(8 * 128 * 256)
-
-    def scaled(g):
-        return (g.astype(F32) * factor).reshape(3, 3, C, HALF)
-
-    return grad_features.reshape(features.shape), scaled(g_one), scaled(g_two)
+    grad_features, two, one = pl.pallas_call(
+        finish,
+        out_shape=(
+            jax.ShapeDtypeStruct((CELLS, C), BF),
+            jax.ShapeDtypeStruct((9, C, HALF), F32),
+            jax.ShapeDtypeStruct((9, C, HALF), F32),
+        ),
+        in_specs=[any_spec] * 3,
+        out_specs=(any_spec, any_spec, any_spec),
+        scratch_shapes=[vmem((6, 3, C, HALF), BF), vmem((6, 3, C, HALF), F32), vmem((CELLS, C), BF), dma((16,))],
+        compiler_params=pltpu.CompilerParams(vmem_limit_bytes=58 * 2**20),
+    )(grad_features, g_two, g_one)
+    shape = (3, 3, C, HALF)
+    return grad_features.reshape(features.shape), one.reshape(shape), two.reshape(shape)
 
 
 def solution(mesh):

time: 61.7 us -> 60.8 us (0.985)
  other arithmetic: 2.98 us -> 0 us
  Pallas kernels: 56.3 us -> 59.2 us
  local copies, waits for them, and re-layouts: 0.97 us -> 0 us
    pallas_call x0 -> x1, Pallas kernels: none -> 3.01 us  [on_device(): pl.pallas_call(finish, out_shape=(jax.ShapeDtypeStruct((CELLS, C), BF), j...]
    mul x1 -> x0, other arithmetic: 2.98 us -> none  [scaled(): return (g.astype(F32) * factor).reshape(3, 3, C, HALF)]
    unnamed x3 -> x0, local copies, waits for them, and re-layouts: 0.97 us -> none
where the time goes in v4:
time: 60.8 us; the launch traced here: 60.6 us
  Pallas kernels  59.2 us (97%)
  between operations  1.47 us (2%)
    pallas_call x1, Pallas kernels, on_device(): pl.pallas_call(body, out_shape=(jax.ShapeDtypeStruct((CELLS, C), BF), jax...  56.1 us
    pallas_call x1, Pallas kernels, on_device(): pl.pallas_call(finish, out_shape=(jax.ShapeDtypeStruct((CELLS, C), BF), j...  3.01 us

profile of v4, /device:TPU:1, one launch (start us, length us, event | category | flops | bytes accessed | tf_op | source)
XLA Modules:
  0.0 60.6 jit_solution(16993033207519997597)
XLA Ops:
  1.3 56.1 %shard_map.103 = (bf16[2048,256]{1,0:T(8,128)(2,1)}, bf16[9,256,128]{2,1,0:T(8,128)(2,1)}, bf16[9,256,128]{2,1,0:T(8,128)(2,1)}) custom-call(bf16[2048,256]{1,0:T(8,128)(2,1)} %bitcast.8, s32[8,256]{1,0:T(8,128)} %bitcast.12, s32[1]{0:T(128)S(6)} %copy.11.bc, f32[3,256]{1,0:T(4,128)} %scale.1, f32[8,256]{1,0:T(8,128)} %bias.1, bf16[2304,128]{1,0:T(8,128)(2,1)} %bitcast.10, ...), custom_call_target="tpu_custom_call" | custom-call | tf_op jit(solution)/shard_map/pallas_call | solution.py:522
  57.4 3.0 %shard_map.104 = (bf16[2048,256]{1,0:T(8,128)(2,1)}, f32[9,256,128]{2,1,0:T(8,128)}, f32[9,256,128]{2,1,0:T(8,128)}) custom-call(bf16[2048,256]{1,0:T(8,128)(2,1)} %get-tuple-element.9.gf, bf16[9,256,128]{2,1,0:T(8,128)(2,1)} %get-tuple-element.10.g_two, bf16[9,256,128]{2,1,0:T(8,128)(2,1)} %get-tuple-element.11.g_one), custom_call_target="tpu_custom_call" | custom-call | tf_op jit(solution)/shard_map/pallas_call | solution.py:583

commit v5 on v4

--- a/solution.py
+++ b/solution.py
@@ -458,16 +458,16 @@
     back_rows(6)
     out_cp = pltpu.make_async_copy(fbuf, gf, load_sem.at[3])
     out_cp.start()
+    stage3(4)
+    stage3(5)
     stage4(1)
-    stage3(4)
     stage4(2)
-    stage3(5)
+    stage4(3)
+    stage4(4)
+    stage4(5)
     stage5(0)
-    stage4(3)
     stage5(1)
-    stage4(4)
     stage5(2)
-    stage4(5)
     stage5(3)
     stage5(4)
     stage5(5)

time: 60.8 us -> 59.9 us (0.985)
  Pallas kernels: 59.2 us -> 58.3 us
    pallas_call x1, Pallas kernels: 56.1 us -> 55.3 us  [on_device(): pl.pallas_call(body, out_shape=(jax.ShapeDtypeStruct((CELLS, C), BF), jax...]
where the time goes in v5:
time: 59.9 us; the launch traced here: 59.8 us
  Pallas kernels  58.3 us (97%)
  between operations  1.47 us (2%)
    pallas_call x1, Pallas kernels, on_device(): pl.pallas_call(body, out_shape=(jax.ShapeDtypeStruct((CELLS, C), BF), jax...  55.3 us
    pallas_call x1, Pallas kernels, on_device(): pl.pallas_call(finish, out_shape=(jax.ShapeDtypeStruct((CELLS, C), BF), j...  3.01 us

profile of v5, /device:TPU:1, one launch (start us, length us, event | category | flops | bytes accessed | tf_op | source)
XLA Modules:
  0.0 59.8 jit_solution(6665723180767565101)
XLA Ops:
  1.3 55.3 %shard_map.103 = (bf16[2048,256]{1,0:T(8,128)(2,1)}, bf16[9,256,128]{2,1,0:T(8,128)(2,1)}, bf16[9,256,128]{2,1,0:T(8,128)(2,1)}) custom-call(bf16[2048,256]{1,0:T(8,128)(2,1)} %bitcast.8, s32[8,256]{1,0:T(8,128)} %bitcast.12, s32[1]{0:T(128)S(6)} %copy.11.bc, f32[3,256]{1,0:T(4,128)} %scale.1, f32[8,256]{1,0:T(8,128)} %bias.1, bf16[2304,128]{1,0:T(8,128)(2,1)} %bitcast.10, ...), custom_call_target="tpu_custom_call" | custom-call | tf_op jit(solution)/shard_map/pallas_call | solution.py:522
  56.6 3.0 %shard_map.104 = (bf16[2048,256]{1,0:T(8,128)(2,1)}, f32[9,256,128]{2,1,0:T(8,128)}, f32[9,256,128]{2,1,0:T(8,128)}) custom-call(bf16[2048,256]{1,0:T(8,128)(2,1)} %get-tuple-element.9.gf, bf16[9,256,128]{2,1,0:T(8,128)(2,1)} %get-tuple-element.10.g_two, bf16[9,256,128]{2,1,0:T(8,128)(2,1)} %get-tuple-element.11.g_one), custom_call_target="tpu_custom_call" | custom-call | tf_op jit(solution)/shard_map/pallas_call | solution.py:583
